TPU v7x, 32 devices: a whole 2x2x4 slice. The times are simulated.
32 devices in a mesh: row: 4 (over y, x), col: 8 (over z, core).
Axes of the slice: x: 2, y: 2, z: 4, core: 2. Of those that a mesh axis runs over, the one named last changes fastest.
Arguments:
- factor: bfloat16 [4, 12, 512, 8, 1, 512], P('row', None, None, 'col'), may hold values from -0.03125 to 0.03125, as said below
- diag_inverse: float32 [4, 2, 1024, 512], P('row'), may hold values from -0.088388348 to 1.5, as said below
- residuals: float32 [256, 12, 4, 512], P('row', None, None, 'col'), may hold values from -6 to 6
Outputs:
- solved: float32 [256, 2, 4, 512], P('col', None, 'row')
- trailing: float32 [256, 10, 4, 512], P('col', None, 'row')
Inputs may be any that keep to these rules, and one draw needn't show every extreme that they name: factor is zero wherever its row block halved (rounded down) is not above its column block halved. `diag_inverse`: each pair's inverse, assembled from its two blocks' columns, is lower triangular with diagonal entries from 0.5 to 1.5.
All inputs are finite; a program needn't handle non-finite values.
Results may differ from a plain program's by a relative error of at most 0.0095.
Values may be sent and summed in bfloat16 or wider, within the bound.
A program may use at most 64 MiB of HBM per device.

v0:
```python
import jax
import jax.numpy as jnp
from jax import lax
from jax.sharding import PartitionSpec as P


def shards(factor, diag_inverse, residuals):
    row_count = lax.axis_size("row")
    col_count = lax.axis_size("col")
    my_row = lax.axis_index("row")
    my_col = lax.axis_index("col")
    local_factor = factor[0, :, :, 0]
    blocks_here = local_factor.shape[0]
    block_width = local_factor.shape[1]
    panel_count = local_factor.shape[2]
    flat_factor = local_factor.reshape(blocks_here, block_width, panel_count * block_width)
    inverses = diag_inverse[0]
    diag_blocks = inverses.shape[0]
    relaid = lax.all_to_all(
        lax.all_to_all(
            residuals.astype(jnp.bfloat16), "row", split_axis=2, concat_axis=0, tiled=True
        ),
        "col",
        split_axis=0,
        concat_axis=3,
        tiled=True,
    ).astype(residuals.dtype)
    own_rhs = relaid[:, :, 0, :]
    slice_width = own_rhs.shape[0]
    walker_total = slice_width * col_count
    pair_total = panel_count * col_count // 2
    known_start = jnp.zeros((walker_total, panel_count * block_width), jnp.bfloat16)
    solved_start = jnp.zeros((slice_width, diag_blocks, block_width), jnp.float32)
    walker_start = my_col * slice_width

    def one_pair(pair_index, loop_state):
        known_blocks, solved_local = loop_state
        first_block = (2 * jnp.asarray(pair_index)).astype(jnp.int32)
        local_block = first_block // row_count
        first_row = first_block % row_count
        is_second = my_row == first_row + 1
        owns = jnp.logical_or(my_row == first_row, is_second)
        block_factor = lax.dynamic_index_in_dim(flat_factor, local_block, 0, keepdims=False)
        partial_value = lax.dot_general(
            known_blocks, block_factor, (((1,), (1,)), ((), ())), preferred_element_type=jnp.float32
        )
        rounded = lax.optimization_barrier(partial_value.astype(jnp.bfloat16)).astype(jnp.float32)
        rhs_block = lax.dynamic_index_in_dim(own_rhs, local_block, 1, keepdims=False)
        inverse = lax.dynamic_index_in_dim(inverses, local_block, 0, keepdims=False)
        rhs_full = lax.dynamic_update_slice(
            jnp.zeros((walker_total, block_width), jnp.float32),
            rhs_block,
            (walker_start, jnp.int32(0)),
        )
        term = lax.dot_general(
            rhs_full - rounded,
            inverse,
            (((1,), (1,)), ((), ())),
            precision=lax.Precision.HIGHEST,
            preferred_element_type=jnp.float32,
        )
        term = jnp.where(owns, term, 0.0)
        pair_solution = lax.psum(term, ("row", "col"))
        own_part = lax.dynamic_slice_in_dim(pair_solution, walker_start, slice_width, 0)
        pair_rounded = pair_solution.astype(jnp.bfloat16)
        own_block = jnp.where(is_second, own_part[:, block_width:], own_part[:, :block_width])
        updated = lax.dynamic_update_index_in_dim(solved_local, own_block, local_block, 1)
        solved_local = jnp.where(owns, updated, solved_local)
        for half in range(2):
            block_index = first_block + half
            placed = pair_rounded[:, half * block_width : (half + 1) * block_width]
            known_blocks = jnp.where(my_col == block_index % col_count, placed, known_blocks)
        return (known_blocks, solved_local)

    known_blocks, solved_local = lax.fori_loop(0, pair_total, one_pair, (known_start, solved_start))
    trail_factor = flat_factor[diag_blocks:]
    trail_summed = lax.psum_scatter(
        lax.dot_general(
            known_blocks, trail_factor, (((1,), (2,)), ((), ())), preferred_element_type=jnp.float32
        ).astype(jnp.bfloat16),
        "col",
        scatter_dimension=0,
        tiled=True,
    ).astype(jnp.float32)
    trailing = own_rhs[:, diag_blocks:, :] - trail_summed
    return (solved_local[:, :, None, :], trailing[:, :, None, :])


def solution(mesh):
    placed = (
        P("row", None, None, "col", None, None),
        P("row", None, None, None),
        P("row", None, None, "col"),
    )
    return jax.shard_map(
        shards,
        mesh=mesh,
        in_specs=placed,
        out_specs=(P("col", None, "row", None), P("col", None, "row", None)),
        check_vma=False,
    )
```

profile of v0, /device:TPU:0, one launch (start us, length us, event | category | flops | bytes accessed | tf_op | source)
XLA Modules:
  0.0 657.8 jit_solution(17106109122414137565)
XLA Ops:
  8.0 1.9 copy.40
  11.1 12.1 %all_to_all.27 = bf16[4,2,24576]{2,1,0:T(2,128)(2,1)S(1)} all-to-all(bf16[4,2,24576]{2,1,0:T(2,128)(2,1)S(1)} %reshape.16), channel_id=1, replica_groups=mesh['row'=4,'col'=8] {'row'}, dimensions={0} | all-to-all | bytes 786432 | tf_op jit(solution)/shard_map/all_to_all | solution.py:20
  23.7 1.3 reshape.18
  25.1 4.9 all-to-all-start.1
  29.9 12.6 %all-to-all-done.1 = bf16[8,2,12288]{2,1,0:T(2,128)(2,1)S(1)} async-done(((bf16[8,2,12288]{2,1,0:T(2,128)(2,1)}), bf16[8,2,12288]{2,1,0:T(2,128)(2,1)S(1)}, u32[]{:S(2)}, u32[]{:S(2)}) %all-to-all-start.1) | async-done | bytes 393248 | tf_op jit(solution)/shard_map/all_to_all | solution.py:19
  43.5 1.1 copy.30
  45.0 560.8 %while.19 = (s32[]{:T(128)}, bf16[256,512]{1,0:T(8,128)(2,1)S(1)}, f32[32,2,512]{2,0,1:T(8,128)S(1)}, s32[]{:T(128)}, s32[]{:T(128)}, /*index=5*/f32[32,12,512]{...) while((s32[]{:T(128)}, bf16[256,512]{1,0:T(8,128)(2,1)S(1)}, ...), condition=%wide.region_2.3_spmd.clone, body=%wide.region_0.2_spmd.clone.sunk | while | flops 1746567168 | bytes 15074070 | solution.py:75
  45.3 1.4 fusion.33
  46.7 1.9 dynamic_update_slice.17
  48.6 6.1 fusion.34
  54.8 126.8 %all-reduce.2.cloned.1.call-done = f32[256,1024]{1,0:T(8,128)} async-done(((f32[256,1024]{1,0:T(8,128)}), f32[256,1024]{1,0:T(8,128)}) %all-reduce.2.cloned.1.call-update) | async-done | bytes 1048592 | tf_op jit(solution)/shard_map/while/body/eval_jaxpr/psum | solution.py:63
  181.7 1.3 convert_element_type.89
  183.1 0.9 fusion.36
  184.3 1.4 fusion.33
  185.7 1.9 dynamic_update_slice.17
  187.7 6.1 fusion.34
  193.9 128.4 %all-reduce.2.cloned.1.call-done = f32[256,1024]{1,0:T(8,128)} async-done(((f32[256,1024]{1,0:T(8,128)}), f32[256,1024]{1,0:T(8,128)}) %all-reduce.2.cloned.1.call-update) | async-done | bytes 1048592 | tf_op jit(solution)/shard_map/while/body/eval_jaxpr/psum | solution.py:63
  322.3 1.3 convert_element_type.89
  324.9 1.4 fusion.33
  326.3 1.9 dynamic_update_slice.17
  328.3 6.1 fusion.34
  334.5 128.4 %all-reduce.2.cloned.1.call-done = f32[256,1024]{1,0:T(8,128)} async-done(((f32[256,1024]{1,0:T(8,128)}), f32[256,1024]{1,0:T(8,128)}) %all-reduce.2.cloned.1.call-update) | async-done | bytes 1048592 | tf_op jit(solution)/shard_map/while/body/eval_jaxpr/psum | solution.py:63
  462.9 1.3 convert_element_type.89
  465.5 1.4 fusion.33
  467.0 1.9 dynamic_update_slice.17
  468.9 6.1 fusion.34
  475.1 128.4 %all-reduce.2.cloned.1.call-done = f32[256,1024]{1,0:T(8,128)} async-done(((f32[256,1024]{1,0:T(8,128)}), f32[256,1024]{1,0:T(8,128)}) %all-reduce.2.cloned.1.call-update) | async-done | bytes 1048592 | tf_op jit(solution)/shard_map/while/body/eval_jaxpr/psum | solution.py:63
  603.5 1.3 convert_element_type.89
  605.9 5.6 fusion.20
  612.3 35.8 %reduce-scatter.2.cloned.1.call-done = bf16[32,10,512]{2,0,1:T(8,128)(2,1)} async-done(((bf16[256,10,512]{2,0,1:T(8,128)(2,1)}), bf16[32,10,512]{2,0,1:T(8,128)(2,1)}) %reduce-scatter.2.cloned.1.call-update) | async-done | bytes 327696 | tf_op jit(solution)/shard_map/reduce_scatter | solution.py:77
  648.1 1.1 fusion.21
  649.2 1.5 copy.34
  (39 shorter events, 8.1 us)
Async XLA Ops:
  25.1 17.4 %all-to-all-start.1 = ((bf16[8,2,12288]{2,1,0:T(2,128)(2,1)}), bf16[8,2,12288]{2,1,0:T(2,128)(2,1)S(1)}, u32[]{:S(2)}, u32[]{:S(2)}) async-start(bf16[8,2,12288]{2,1,0:T(2,128)(2,1)} %reshape.18), calls=%async_computation.1 | async-start | bytes 786432 | tf_op jit(solution)/shard_map/all_to_all | solution.py:19
  45.0 136.6 %all-reduce.2.cloned.1.call-start = ((), (), s32[]{:S(2)}) async-start(), calls=%async_computation.4 | async-start | bytes 2097152 | tf_op jit(solution)/shard_map/while/body/eval_jaxpr/psum | solution.py:63
  184.0 138.2 %all-reduce.2.cloned.1.call-start = ((), (), s32[]{:S(2)}) async-start(), calls=%async_computation.4 | async-start | bytes 2097152 | tf_op jit(solution)/shard_map/while/body/eval_jaxpr/psum | solution.py:63
  324.7 138.2 %all-reduce.2.cloned.1.call-start = ((), (), s32[]{:S(2)}) async-start(), calls=%async_computation.4 | async-start | bytes 2097152 | tf_op jit(solution)/shard_map/while/body/eval_jaxpr/psum | solution.py:63
  465.3 138.2 %all-reduce.2.cloned.1.call-start = ((), (), s32[]{:S(2)}) async-start(), calls=%async_computation.4 | async-start | bytes 2097152 | tf_op jit(solution)/shard_map/while/body/eval_jaxpr/psum | solution.py:63
  605.9 42.2 %reduce-scatter.2.cloned.1.call-start = ((), (), s32[]{:S(2)}) async-start(), calls=%async_computation.3 | async-start | bytes 2949120 | tf_op jit(solution)/shard_map/reduce_scatter | solution.py:77
Sparse Core Ops, SparseCore 0:
  54.9 126.7 all-reduce.1
  193.9 128.3 all-reduce.1
  334.5 128.3 all-reduce.1
  475.1 128.3 all-reduce.1
Sparse Core Ops, SparseCore 1:
  611.6 36.5 reduce-scatter.1
where the time goes:
time: 659 us; the launch traced here: 658 us
  waiting for transfers between devices  561 us (85%)
  matrix products  35.5 us (5%)
  local copies, waits for them, and re-layouts  17.9 us (3%)
  between operations  15.2 us (2%)
  blocking collectives  12.1 us (2%)
  other arithmetic  10.6 us (2%)
    psum x4, waiting for transfers between devices, one_pair(): pair_solution = lax.psum(term, ('row', 'col'))  512 us
    reduce_scatter x1, waiting for transfers between devices, shards(): lax.psum_scatter(lax.dot_general(known_blocks, trail_factor, (((1,), (2,)...  35.8 us
    dot_general x4, matrix products, one_pair(): lax.dot_general(rhs_full - rounded, inverse, (((1,), (1,)), ((), ())), pr...  24.5 us
  transfers between devices with their start and end apart: 6, of which 6 were waited for; matrix products, arithmetic and copies ran while one was open for 0% of the time, Pallas kernels for 0%

commit v1 on v0

--- a/solution.py
+++ b/solution.py
@@ -60,7 +60,7 @@
             preferred_element_type=jnp.float32,
         )
         term = jnp.where(owns, term, 0.0)
-        pair_solution = lax.psum(term, ("row", "col"))
+        pair_solution = lax.psum(lax.psum(term, "col"), "row")
         own_part = lax.dynamic_slice_in_dim(pair_solution, walker_start, slice_width, 0)
         pair_rounded = pair_solution.astype(jnp.bfloat16)
         own_block = jnp.where(is_second, own_part[:, block_width:], own_part[:, :block_width])

time: 659 us -> 597 us (0.906)
  waiting for transfers between devices: 561 us -> 499 us
    psum x4 -> x8, waiting for transfers between devices: 512 us -> 449 us  [one_pair(): pair_solution = lax.psum(lax.psum(term, 'col'), 'row')]
  transfers between devices with their start and end apart: 6 -> 10, of which waited for: 6 -> 10; matrix products, arithmetic and copies ran while one was open for 0% -> 0% of each run, Pallas kernels for 0% -> 0%
where the time goes in v1:
time: 597 us; the launch traced here: 596 us
  waiting for transfers between devices  499 us (84%)
  matrix products  35.6 us (6%)
  local copies, waits for them, and re-layouts  17.9 us (3%)
  between operations  15.5 us (3%)
  blocking collectives  12.1 us (2%)
  other arithmetic  10.6 us (2%)
    psum x8, waiting for transfers between devices, one_pair(): pair_solution = lax.psum(lax.psum(term, 'col'), 'row')  449 us
    reduce_scatter x1, waiting for transfers between devices, shards(): lax.psum_scatter(lax.dot_general(known_blocks, trail_factor, (((1,), (2,)...  36.8 us
    dot_general x4, matrix products, one_pair(): lax.dot_general(rhs_full - rounded, inverse, (((1,), (1,)), ((), ())), pr...  24.5 us
    all_to_all x1, waiting for transfers between devices, shards(): lax.all_to_all(lax.all_to_all(residuals.astype(jnp.bfloat16), 'row', spli...  12.6 us
    all_to_all x1, blocking collectives, shards(): lax.all_to_all(residuals.astype(jnp.bfloat16), 'row', split_axis=2, conca...  12.1 us
  transfers between devices with their start and end apart: 10, of which 10 were waited for; matrix products, arithmetic and copies ran while one was open for 0% of the time, Pallas kernels for 0%

profile of v1, /device:TPU:0, one launch (start us, length us, event | category | flops | bytes accessed | tf_op | source)
XLA Modules:
  0.0 596.3 jit_solution(16061215601669823134)
XLA Ops:
  8.0 1.9 copy.40
  11.1 12.1 %all_to_all.27 = bf16[4,2,24576]{2,1,0:T(2,128)(2,1)S(1)} all-to-all(bf16[4,2,24576]{2,1,0:T(2,128)(2,1)S(1)} %reshape.16), channel_id=1, replica_groups=mesh['row'=4,'col'=8] {'row'}, dimensions={0} | all-to-all | bytes 786432 | tf_op jit(solution)/shard_map/all_to_all | solution.py:20
  23.7 1.3 reshape.18
  25.1 4.9 all-to-all-start.1
  29.9 12.6 %all-to-all-done.1 = bf16[8,2,12288]{2,1,0:T(2,128)(2,1)S(1)} async-done(((bf16[8,2,12288]{2,1,0:T(2,128)(2,1)}), bf16[8,2,12288]{2,1,0:T(2,128)(2,1)S(1)}, u32[]{:S(2)}, u32[]{:S(2)}) %all-to-all-start.1) | async-done | bytes 393248 | tf_op jit(solution)/shard_map/all_to_all | solution.py:19
  45.0 498.0 %while.19 = (s32[]{:T(128)}, bf16[256,512]{1,0:T(8,128)(2,1)S(1)}, f32[32,2,512]{2,0,1:T(8,128)S(1)}, s32[]{:T(128)}, s32[]{:T(128)}, /*index=5*/f32[32,12,512]{...) while((s32[]{:T(128)}, bf16[256,512]{1,0:T(8,128)(2,1)S(1)}, ...), condition=%wide.region_3.4_spmd.clone, body=%wide.region_0.3_spmd.clone.sunk | while | flops 1746829312 | bytes 21365560 | solution.py:75
  45.3 1.4 fusion.33
  46.7 1.9 dynamic_update_slice.17
  48.7 6.1 %fusion.34 = f32[256,1024]{1,0:T(8,128)} fusion(f32[2,1024,512]{2,1,0:T(8,128)} %get-tuple-element.466, s32[]{:T(128)S(6)} %select_n.283, f32[256,512]{0,1:T(8,128)S(1)} %dynamic_update_slice.17, bf16[256,512]{0,1:T(8,128)(2,1)S(1)} %fusion.33, pred[]{:T(512)S(6)} %or.13), kind=kOutput, calls=%fused_computation.3.clone.1 | convolution fusion | flops 1611137024 | bytes 3932165 | tf_op jit(solution)/shard_map/while/body/eval_jaxpr/dot_general | solution.py:55
  54.8 55.8 %all-reduce.3.cloned.1.call-done = f32[256,1024]{1,0:T(8,128)} async-done(((f32[256,1024]{1,0:T(8,128)}), f32[256,1024]{1,0:T(8,128)}) %all-reduce.3.cloned.1.call-update) | async-done | bytes 1048592 | tf_op jit(solution)/shard_map/while/body/eval_jaxpr/psum | solution.py:63
  110.7 54.5 %all-reduce.5.cloned.1.call-done = f32[256,1024]{1,0:T(8,128)} async-done(((f32[256,1024]{1,0:T(8,128)}), f32[256,1024]{1,0:T(8,128)}) %all-reduce.5.cloned.1.call-update) | async-done | bytes 1048592 | tf_op jit(solution)/shard_map/while/body/eval_jaxpr/psum | solution.py:63
  165.3 1.3 convert_element_type.89
  167.9 1.4 fusion.33
  169.3 1.9 dynamic_update_slice.17
  171.2 6.1 %fusion.34 = f32[256,1024]{1,0:T(8,128)} fusion(f32[2,1024,512]{2,1,0:T(8,128)} %get-tuple-element.466, s32[]{:T(128)S(6)} %select_n.283, f32[256,512]{0,1:T(8,128)S(1)} %dynamic_update_slice.17, bf16[256,512]{0,1:T(8,128)(2,1)S(1)} %fusion.33, pred[]{:T(512)S(6)} %or.13), kind=kOutput, calls=%fused_computation.3.clone.1 | convolution fusion | flops 1611137024 | bytes 3932165 | tf_op jit(solution)/shard_map/while/body/eval_jaxpr/dot_general | solution.py:55
  177.4 58.5 %all-reduce.3.cloned.1.call-done = f32[256,1024]{1,0:T(8,128)} async-done(((f32[256,1024]{1,0:T(8,128)}), f32[256,1024]{1,0:T(8,128)}) %all-reduce.3.cloned.1.call-update) | async-done | bytes 1048592 | tf_op jit(solution)/shard_map/while/body/eval_jaxpr/psum | solution.py:63
  236.0 54.4 %all-reduce.5.cloned.1.call-done = f32[256,1024]{1,0:T(8,128)} async-done(((f32[256,1024]{1,0:T(8,128)}), f32[256,1024]{1,0:T(8,128)}) %all-reduce.5.cloned.1.call-update) | async-done | bytes 1048592 | tf_op jit(solution)/shard_map/while/body/eval_jaxpr/psum | solution.py:63
  290.4 1.3 convert_element_type.89
  293.0 1.4 fusion.33
  294.4 1.9 dynamic_update_slice.17
  296.3 6.1 %fusion.34 = f32[256,1024]{1,0:T(8,128)} fusion(f32[2,1024,512]{2,1,0:T(8,128)} %get-tuple-element.466, s32[]{:T(128)S(6)} %select_n.283, f32[256,512]{0,1:T(8,128)S(1)} %dynamic_update_slice.17, bf16[256,512]{0,1:T(8,128)(2,1)S(1)} %fusion.33, pred[]{:T(512)S(6)} %or.13), kind=kOutput, calls=%fused_computation.3.clone.1 | convolution fusion | flops 1611137024 | bytes 3932165 | tf_op jit(solution)/shard_map/while/body/eval_jaxpr/dot_general | solution.py:55
  302.5 58.4 %all-reduce.3.cloned.1.call-done = f32[256,1024]{1,0:T(8,128)} async-done(((f32[256,1024]{1,0:T(8,128)}), f32[256,1024]{1,0:T(8,128)}) %all-reduce.3.cloned.1.call-update) | async-done | bytes 1048592 | tf_op jit(solution)/shard_map/while/body/eval_jaxpr/psum | solution.py:63
  361.0 54.4 %all-reduce.5.cloned.1.call-done = f32[256,1024]{1,0:T(8,128)} async-done(((f32[256,1024]{1,0:T(8,128)}), f32[256,1024]{1,0:T(8,128)}) %all-reduce.5.cloned.1.call-update) | async-done | bytes 1048592 | tf_op jit(solution)/shard_map/while/body/eval_jaxpr/psum | solution.py:63
  418.0 1.4 fusion.33
  419.5 1.9 dynamic_update_slice.17
  421.4 6.1 %fusion.34 = f32[256,1024]{1,0:T(8,128)} fusion(f32[2,1024,512]{2,1,0:T(8,128)} %get-tuple-element.466, s32[]{:T(128)S(6)} %select_n.283, f32[256,512]{0,1:T(8,128)S(1)} %dynamic_update_slice.17, bf16[256,512]{0,1:T(8,128)(2,1)S(1)} %fusion.33, pred[]{:T(512)S(6)} %or.13), kind=kOutput, calls=%fused_computation.3.clone.1 | convolution fusion | flops 1611137024 | bytes 3932165 | tf_op jit(solution)/shard_map/while/body/eval_jaxpr/dot_general | solution.py:55
  427.6 58.5 %all-reduce.3.cloned.1.call-done = f32[256,1024]{1,0:T(8,128)} async-done(((f32[256,1024]{1,0:T(8,128)}), f32[256,1024]{1,0:T(8,128)}) %all-reduce.3.cloned.1.call-update) | async-done | bytes 1048592 | tf_op jit(solution)/shard_map/while/body/eval_jaxpr/psum | solution.py:63
  486.2 54.5 %all-reduce.5.cloned.1.call-done = f32[256,1024]{1,0:T(8,128)} async-done(((f32[256,1024]{1,0:T(8,128)}), f32[256,1024]{1,0:T(8,128)}) %all-reduce.5.cloned.1.call-update) | async-done | bytes 1048592 | tf_op jit(solution)/shard_map/while/body/eval_jaxpr/psum | solution.py:63
  540.7 1.3 convert_element_type.89
  543.1 5.6 fusion.20
  549.5 36.8 %reduce-scatter.2.cloned.1.call-done = bf16[32,10,512]{2,0,1:T(8,128)(2,1)} async-done(((bf16[256,10,512]{2,0,1:T(8,128)(2,1)}), bf16[32,10,512]{2,0,1:T(8,128)(2,1)}) %reduce-scatter.2.cloned.1.call-update) | async-done | bytes 327696 | tf_op jit(solution)/shard_map/reduce_scatter | solution.py:77
  587.3 1.5 copy.34
  (51 shorter events, 12.7 us)
Async XLA Ops:
  25.1 17.4 %all-to-all-start.1 = ((bf16[8,2,12288]{2,1,0:T(2,128)(2,1)}), bf16[8,2,12288]{2,1,0:T(2,128)(2,1)S(1)}, u32[]{:S(2)}, u32[]{:S(2)}) async-start(bf16[8,2,12288]{2,1,0:T(2,128)(2,1)} %reshape.18), calls=%async_computation.1 | async-start | bytes 786432 | tf_op jit(solution)/shard_map/all_to_all | solution.py:19
  45.0 65.6 %all-reduce.3.cloned.1.call-start = ((), (), s32[]{:S(2)}) async-start(), calls=%async_computation.4 | async-start | bytes 2097152 | tf_op jit(solution)/shard_map/while/body/eval_jaxpr/psum | solution.py:63
  54.8 110.5 %all-reduce.5.cloned.1.call-start = ((), (), s32[]{:S(2)}) async-start(), calls=%async_computation.5 | async-start | bytes 2097152 | tf_op jit(solution)/shard_map/while/body/eval_jaxpr/psum | solution.py:63
  167.6 68.3 %all-reduce.3.cloned.1.call-start = ((), (), s32[]{:S(2)}) async-start(), calls=%async_computation.4 | async-start | bytes 2097152 | tf_op jit(solution)/shard_map/while/body/eval_jaxpr/psum | solution.py:63
  177.4 113.0 %all-reduce.5.cloned.1.call-start = ((), (), s32[]{:S(2)}) async-start(), calls=%async_computation.5 | async-start | bytes 2097152 | tf_op jit(solution)/shard_map/while/body/eval_jaxpr/psum | solution.py:63
  292.7 68.2 %all-reduce.3.cloned.1.call-start = ((), (), s32[]{:S(2)}) async-start(), calls=%async_computation.4 | async-start | bytes 2097152 | tf_op jit(solution)/shard_map/while/body/eval_jaxpr/psum | solution.py:63
  302.5 112.9 %all-reduce.5.cloned.1.call-start = ((), (), s32[]{:S(2)}) async-start(), calls=%async_computation.5 | async-start | bytes 2097152 | tf_op jit(solution)/shard_map/while/body/eval_jaxpr/psum | solution.py:63
  417.8 68.3 %all-reduce.3.cloned.1.call-start = ((), (), s32[]{:S(2)}) async-start(), calls=%async_computation.4 | async-start | bytes 2097152 | tf_op jit(solution)/shard_map/while/body/eval_jaxpr/psum | solution.py:63
  427.6 113.2 %all-reduce.5.cloned.1.call-start = ((), (), s32[]{:S(2)}) async-start(), calls=%async_computation.5 | async-start | bytes 2097152 | tf_op jit(solution)/shard_map/while/body/eval_jaxpr/psum | solution.py:63
  543.1 43.2 %reduce-scatter.2.cloned.1.call-start = ((), (), s32[]{:S(2)}) async-start(), calls=%async_computation.3 | async-start | bytes 2949120 | tf_op jit(solution)/shard_map/reduce_scatter | solution.py:77
Sparse Core Ops, SparseCore 0:
  54.9 55.7 all-reduce.2
  113.7 51.4 all-reduce.4
  177.5 58.3 all-reduce.2
  238.8 51.4 all-reduce.4
  302.6 58.3 all-reduce.2
  363.9 51.4 all-reduce.4
  427.7 58.3 all-reduce.2
  489.2 51.4 all-reduce.4
Sparse Core Ops, SparseCore 1:
  548.8 37.4 reduce-scatter.1
